TPU v7x, 256 devices: a whole 4x4x8 slice. The times are simulated.
256 devices in a mesh: blk: 16 (over x_hi, z), grp: 16 (over x_lo, y, core).
Axes of the slice: x: 4 (x_hi: 2, x_lo: 2; x = x_hi * 2 + x_lo), y: 4, z: 8, core: 2. Of those that a mesh axis runs over, the one named last changes fastest.
Arguments:
- queries: bfloat16 [16, 2048, 4096], P('grp', 'blk'), may hold values from -72 to 72
- question_pos: int32 [16, 2048], P('grp', 'blk'), may hold values from 0 to 1023
- cache_limit: int32 [16, 2048], P('grp', 'blk'), may hold values from 256 to 1024
- cache: bfloat16 [1024, 2048], P('blk'), may hold values from -6 to 6
- prefix: bfloat16 [2, 8, 128, 128], replicated, may hold values from -6 to 6
Outputs:
- prefix_step: float32 [2048, 128], P(('blk', 'grp'))
- row_error: float32 [16, 2048], P('grp', 'blk')
All inputs are finite; a program needn't handle non-finite values.
Results may differ from a plain program's by a relative error of at most 0.012.
The roundings to bfloat16 on the way count: a program that leaves them out, or rounds other values in their place, can miss the bound.
Values may be sent and summed in bfloat16 or wider, within the bound.
A program may use at most 64 MiB of HBM per device.

v0:
```python
import math

import jax
import jax.numpy as jnp
from jax import lax
from jax.sharding import PartitionSpec as P

rope_base = 500000.0
neg_fill = -1e30
norm_eps = 1e-06


def sent_together(arrays, axis, split_dim, concat_dim, along):
    both = jnp.concatenate(arrays, axis=along)
    result, at, outs = (
        lax.all_to_all(both, axis, split_axis=split_dim, concat_axis=concat_dim, tiled=True),
        0,
        [],
    )
    for a in arrays:
        outs.append(lax.slice_in_dim(result, at, at + a.shape[along], axis=along))
        at += a.shape[along]
    return tuple(outs)


def rotate(vectors, positions):
    halfway = vectors.shape[-1] // 2
    frequency = rope_base ** (-jnp.arange(halfway, dtype=jnp.float32) / halfway)
    angles = positions.astype(jnp.float32)[:, None] * frequency[None, :]
    cosine = jnp.cos(angles)[:, None, :]
    sine_part = jnp.sin(angles)[:, None, :]
    values = vectors.astype(jnp.float32)
    leading = values[..., :halfway]
    trailing = values[..., halfway:]
    turned = jnp.concatenate(
        [leading * cosine - trailing * sine_part, trailing * cosine + leading * sine_part], axis=-1
    )
    return turned.astype(jnp.bfloat16)


def absorb(teacher_q, limits, running, block_rows, offset):
    maxima, totals, mixture = running
    heads_kv = teacher_q.shape[1]
    head_width = teacher_q.shape[3]
    key_width = heads_kv * head_width
    block_size = block_rows.shape[0]
    key_part = block_rows[:, :key_width].reshape(block_size, heads_kv, head_width)
    value_part = block_rows[:, key_width:].reshape(block_size, heads_kv, head_width)
    scores = jnp.einsum(
        "rcgd,jcd->rcgj", teacher_q, key_part, preferred_element_type=jnp.float32
    ) * head_width ** (-0.5)
    visible = ((offset + jnp.arange(block_size, dtype=jnp.int32))[None, :] < limits[:, None])[
        :, None, None, :
    ]
    masked = jnp.where(visible, scores, neg_fill)
    renewed = jnp.maximum(maxima, jnp.max(masked, axis=-1))
    raised = jnp.where(visible, jnp.exp(masked - renewed[..., None]), 0.0)
    factor = jnp.exp(maxima - renewed)
    totals = totals * factor + jnp.sum(raised, axis=-1)
    mixture = mixture * factor[..., None] + jnp.einsum(
        "rcgj,jcd->rcgd",
        raised.astype(jnp.bfloat16),
        value_part,
        preferred_element_type=jnp.float32,
    )
    return (renewed, totals, mixture)


def starting(teacher_q):
    grouped_shape = teacher_q.shape[:3]
    return (
        jnp.full(grouped_shape, neg_fill, jnp.float32),
        jnp.zeros(grouped_shape, jnp.float32),
        jnp.zeros(teacher_q.shape, jnp.float32),
    )


def student_block(student_q, prefix, target):
    row_count = student_q.shape[0]
    heads_kv = prefix.shape[1]
    head_width = prefix.shape[3]
    grouped = student_q.reshape(row_count, heads_kv, -1, head_width)
    scaling = head_width ** (-0.5)
    scores = (
        jnp.einsum("rcgd,cpd->rcgp", grouped, prefix[0], preferred_element_type=jnp.float32)
        * scaling
    )
    raised = jnp.exp(scores - jnp.max(scores, axis=-1, keepdims=True))
    weights = raised / jnp.sum(raised, axis=-1, keepdims=True)
    rounded = weights.astype(jnp.bfloat16)
    output = jnp.einsum("rcgp,cpd->rcgd", rounded, prefix[1], preferred_element_type=jnp.float32)
    difference = output - target
    cotangent = difference.astype(jnp.bfloat16)
    grad_values = jnp.einsum(
        "rcgp,rcgd->cpd", rounded, cotangent, preferred_element_type=jnp.float32
    )
    along_values = jnp.einsum(
        "rcgd,cpd->rcgp", cotangent, prefix[1], preferred_element_type=jnp.float32
    )
    inner_sum = jnp.sum(weights * along_values, axis=-1, keepdims=True)
    score_grad = (weights * (along_values - inner_sum) * scaling).astype(jnp.bfloat16)
    grad_keys = jnp.einsum(
        "rcgp,rcgd->cpd", score_grad, grouped, preferred_element_type=jnp.float32
    )
    diff_sq = jnp.sum(difference * difference, axis=(1, 2, 3))
    target_sq = jnp.sum(target * target, axis=(1, 2, 3))
    return (diff_sq, target_sq, jnp.stack([grad_keys, grad_values]))


def shards(queries, question_pos, cache_limit, cache, prefix):
    heads_kv = prefix.shape[1]
    head_width = prefix.shape[3]
    row_count = queries.shape[1]
    features = queries.shape[2]
    vectors = queries[0].reshape(row_count, -1, head_width)
    limits = cache_limit[0]
    teacher_q = rotate(vectors, limits + question_pos[0]).reshape(
        row_count, heads_kv, -1, head_width
    )
    student_q = rotate(vectors, prefix.shape[2] + question_pos[0])
    shard_rows = cache.shape[0]
    cycle_size = lax.axis_size("blk")
    repeats = cycle_size // heads_kv
    part_rows = row_count // repeats
    per_head = teacher_q.shape[2]
    wide = per_head * head_width
    head_index = lax.axis_index("blk") // repeats

    def arrange(values):
        return (
            values.reshape(repeats, part_rows, heads_kv, wide)
            .transpose(2, 0, 1, 3)
            .reshape(cycle_size, part_rows, wide)
        )

    sent_teacher = arrange(teacher_q)
    sent_student = arrange(student_q)
    got_teacher, got_student = sent_together((sent_teacher, sent_student), "blk", 0, 1, 2)
    sent_limits = jnp.broadcast_to(
        limits.reshape(1, repeats, part_rows), (heads_kv, repeats, part_rows)
    ).reshape(cycle_size, part_rows)
    got_limits = lax.all_to_all(sent_limits, "blk", split_axis=0, concat_axis=1, tiled=True)[0]
    key_width = heads_kv * head_width
    paired = jnp.concatenate(
        [
            cache[:, :key_width].reshape(shard_rows, heads_kv, head_width),
            cache[:, key_width:].reshape(shard_rows, heads_kv, head_width),
        ],
        axis=-1,
    )
    sent_cache = jnp.repeat(paired.transpose(1, 0, 2), repeats, axis=0)
    head_cache = lax.all_to_all(sent_cache, "blk", split_axis=0, concat_axis=1, tiled=True)[0]
    total_rows = got_teacher.shape[1]
    local_teacher = got_teacher[0].reshape(total_rows, 1, per_head, head_width)
    positions_all = head_cache.shape[0]
    step_rows = math.gcd(positions_all, 512)
    stacked = head_cache.reshape(positions_all // step_rows, step_rows, 2 * head_width)
    starts = step_rows * jnp.arange(positions_all // step_rows, dtype=jnp.int32)

    def advance(current, element):
        return (absorb(local_teacher, got_limits, current, element[0], element[1]), None)

    running, unused = lax.scan(advance, starting(local_teacher), (stacked, starts))
    maxima, totals, mixture = running
    target = mixture / totals[..., None]
    head_prefix = lax.dynamic_slice_in_dim(prefix, head_index, 1, 1)
    local_student = got_student[0].reshape(total_rows, per_head, head_width)
    part_diff, part_target, compact = student_block(local_student, head_prefix, target)
    back_diff, back_target = sent_together(
        (part_diff.reshape(cycle_size, part_rows), part_target.reshape(cycle_size, part_rows)),
        "blk",
        0,
        0,
        1,
    )
    diff_sq = jnp.sum(back_diff.reshape(heads_kv, repeats, part_rows), axis=0).reshape(row_count)
    target_sq = jnp.sum(back_target.reshape(heads_kv, repeats, part_rows), axis=0).reshape(
        row_count
    )
    gradient = lax.dynamic_update_slice_in_dim(
        jnp.zeros((2, heads_kv) + compact.shape[2:], jnp.float32), compact, head_index, 1
    )
    row_error = jnp.sqrt(diff_sq / features) / jnp.sqrt(target_sq / features + norm_eps)
    flattened = gradient.reshape(-1, head_width)
    summed = lax.psum(flattened, ("blk", "grp"))
    mean_square = jnp.mean(summed * summed)
    share_rows = summed.shape[0] // lax.axis_size(("blk", "grp"))
    own_rows = lax.dynamic_slice_in_dim(
        summed, lax.axis_index(("blk", "grp")) * share_rows, share_rows, 0
    )
    prefix_step = own_rows / jnp.sqrt(mean_square + norm_eps)
    return (prefix_step, row_error[None, :])


def solution(mesh):
    return jax.shard_map(
        shards,
        mesh=mesh,
        in_specs=(P("grp", "blk", None), P("grp", "blk"), P("grp", "blk"), P("blk", None), P()),
        out_specs=(P(("blk", "grp"), None), P("grp", "blk")),
        check_vma=False,
    )
```

profile of v0, /device:TPU:1, one launch (start us, length us, event | category | flops | bytes accessed | tf_op | source)
XLA Modules:
  0.0 424.6 jit_solution(797250310668742604)
XLA Ops:
  9.7 11.6 %all-to-all-start.1 = ((s32[16,1,64]{2,1,0:T(1,128)}), s32[16,1,64]{2,1,0:T(1,128)S(1)}, u32[]{:S(2)}, u32[]{:S(2)}) async-start(s32[16,1,64]{2,1,0:T(1,128)} %bitcast.19), calls=%async_computation.1 | async-start | bytes 16384 | tf_op jit(solution)/shard_map/all_to_all | solution.py:142
  25.0 2.1 pad_maximum_fusion.1
  27.1 1.7 convert_element_type.53
  32.0 1.6 pad_maximum_fusion
  33.7 9.2 %all-to-all-start = ((bf16[16,64,1024]{2,1,0:T(8,128)(2,1)}), bf16[16,64,1024]{2,1,0:T(8,128)(2,1)S(1)}, u32[]{:S(2)}, u32[]{:S(2)}) async-start(bf16[16,64,1024]{2,1,0:T(8,128)(2,1)} %pad_maximum_fusion), calls=%async_computation | async-start | bytes 4194304 | tf_op jit(solution)/shard_map/all_to_all | solution.py:16
  43.0 48.1 %all-to-all-done = bf16[16,64,1024]{2,1,0:T(8,128)(2,1)S(1)} async-done(((bf16[16,64,1024]{2,1,0:T(8,128)(2,1)}), bf16[16,64,1024]{2,1,0:T(8,128)(2,1)S(1)}, u32[]{:S(2)}, u32[]{:S(2)}) %all-to-all-start) | async-done | bytes 2097184 | tf_op jit(solution)/shard_map/all_to_all | solution.py:16
  92.0 7.7 %all-to-all-start.2 = ((bf16[16,64,256]{2,1,0:T(8,128)(2,1)}), bf16[16,64,256]{2,1,0:T(8,128)(2,1)S(1)}, u32[]{:S(2)}, u32[]{:S(2)}) async-start(bf16[16,64,256]{2,1,0:T(8,128)(2,1)} %bitcast.215), calls=%async_computation.2 | async-start | bytes 1048576 | tf_op jit(solution)/shard_map/all_to_all | solution.py:152
  100.7 1.5 fusion.44
  102.2 1.5 copy.65
  104.4 9.6 %all-to-all-done.2 = bf16[16,64,256]{2,1,0:T(8,128)(2,1)S(1)} async-done(((bf16[16,64,256]{2,1,0:T(8,128)(2,1)}), bf16[16,64,256]{2,1,0:T(8,128)(2,1)S(1)}, u32[]{:S(2)}, u32[]{:S(2)}) %all-to-all-start.2) | async-done | bytes 524320 | tf_op jit(solution)/shard_map/all_to_all | solution.py:152
  113.9 32.8 %while.15 = (s32[]{:T(128)}, f32[1024,1,4]{0,2,1:T(4,128)S(1)}, f32[1024,1,4]{0,2,1:T(4,128)S(1)}, f32[1024,1,4,128]{0,3,2,1:T(8,128)}, s32[2]{0:T(128)S(1)}, /*...) while((s32[]{:T(128)}, f32[1024,1,4]{0,2,1:T(4,128)S(1)}, ...), condition=%wide.region_5.6_spmd.clone, body=%wide.region_2.5_spmd.clone.sunk | while | flops 1103127040 | bytes 67117216 | solution.py:163
  115.6 4.8 %fusion.53 = (f32[1024,4]{0,1:T(4,128)S(1)}, f32[512,1024,4]{1,0,2:T(8,128)}) fusion(pred[1024,512]{0,1:T(8,128)(4,1)S(1)} %broadcast_compare_fusion.2, bf16[1024,1,4,128]{3,0,2,1:T(8,128)(2,1)S(1)} %get-tuple-element.233, bf16[512,256]{1,0:T(8,128)(2,1)S(1)} %dynamic-slice_bitcast_fusion.7), kind=kOutput, calls=%fused_computation.2.clone.1 | convolution fusion | flops 543158272 | bytes 10108928 | tf_op jit(solution)/shard_map/while/body/eval_jaxpr/rcgd,jcd->rcgj/dot_general | solution.py:49
  120.4 7.4 %bitcast_add_fusion.5 = f32[1024,1,4,128]{0,3,2,1:T(8,128)} fusion(f32[1024,1,4,128]{0,3,2,1:T(8,128)} %get-tuple-element.219, f32[512,1024,4]{1,0,2:T(8,128)} %get-tuple-element.204, f32[1024,4]{0,1:T(4,128)S(1)} %bitcast.204, pred[1024,512]{0,1:T(8,128)(4,1)S(1)} %broadcast_compare_fusion.2, f32[1024,4]{0,1:T(4,128)S(1)} %get-tuple-element.205, ...), kind=kOutput, calls=%fused_computation.8.clone.1 | convolution fusion | flops 548929536 | bytes 13271041 | tf_op jit(solution)/shard_map/while/body/eval_jaxpr/rcgj,jcd->rcgd/dot_general | solution.py:60
  127.9 2.1 fusion.55
  131.7 4.8 %fusion.53 = (f32[1024,4]{0,1:T(4,128)S(1)}, f32[512,1024,4]{1,0,2:T(8,128)}) fusion(pred[1024,512]{0,1:T(8,128)(4,1)S(1)} %broadcast_compare_fusion.2, bf16[1024,1,4,128]{3,0,2,1:T(8,128)(2,1)S(1)} %get-tuple-element.233, bf16[512,256]{1,0:T(8,128)(2,1)S(1)} %dynamic-slice_bitcast_fusion.7), kind=kOutput, calls=%fused_computation.2.clone.1 | convolution fusion | flops 543158272 | bytes 10108928 | tf_op jit(solution)/shard_map/while/body/eval_jaxpr/rcgd,jcd->rcgj/dot_general | solution.py:49
  136.5 8.0 %bitcast_add_fusion.5 = f32[1024,1,4,128]{0,3,2,1:T(8,128)} fusion(f32[1024,1,4,128]{0,3,2,1:T(8,128)} %get-tuple-element.219, f32[512,1024,4]{1,0,2:T(8,128)} %get-tuple-element.204, f32[1024,4]{0,1:T(4,128)S(1)} %bitcast.204, pred[1024,512]{0,1:T(8,128)(4,1)S(1)} %broadcast_compare_fusion.2, f32[1024,4]{0,1:T(4,128)S(1)} %get-tuple-element.205, ...), kind=kOutput, calls=%fused_computation.8.clone.1 | convolution fusion | flops 548929536 | bytes 13271041 | tf_op jit(solution)/shard_map/while/body/eval_jaxpr/rcgj,jcd->rcgd/dot_general | solution.py:60
  144.6 2.1 fusion.55
  146.7 2.4 copy.64
  152.9 2.0 fusion.15
  155.6 2.6 convolution_bitcast_fusion.1
  160.1 6.3 %all-to-all-start.3 = ((f32[16,1,128]{2,1,0:T(1,128)}), f32[16,1,128]{2,1,0:T(1,128)S(1)}, u32[]{:S(2)}, u32[]{:S(2)}) async-start(f32[16,1,128]{2,1,0:T(1,128)} %bitcast.35), calls=%async_computation.3 | async-start | bytes 16384 | tf_op jit(solution)/shard_map/all_to_all | solution.py:16
  166.4 8.6 %all-to-all-done.3 = f32[16,1,128]{2,1,0:T(1,128)S(1)} async-done(((f32[16,1,128]{2,1,0:T(1,128)}), f32[16,1,128]{2,1,0:T(1,128)S(1)}, u32[]{:S(2)}, u32[]{:S(2)}) %all-to-all-start.3) | async-done | bytes 8224 | tf_op jit(solution)/shard_map/all_to_all | solution.py:16
  175.8 237.9 %all-reduce.2.cloned.1.call-done = f32[2048,128]{1,0:T(8,128)} async-done(((f32[2048,128]{1,0:T(8,128)}), f32[2048,128]{1,0:T(8,128)}) %all-reduce.2.cloned.1.call-update) | async-done | bytes 1048592 | tf_op jit(solution)/shard_map/psum | solution.py:185
  413.7 2.1 multiply_reduce_fusion.2
  (76 shorter events, 23.6 us)
Async XLA Ops:
  7.2 142.3 %copy-start = (bf16[2,8,128,128]{3,2,1,0:T(8,128)(2,1)S(1)}, bf16[2,8,128,128]{3,2,1,0:T(8,128)(2,1)}, u32[]{:S(2)}) copy-start(bf16[2,8,128,128]{3,2,1,0:T(8,128)(2,1)} %param.11) | copy-start | bytes 1572868
  9.7 23.9 %all-to-all-start.1 = ((s32[16,1,64]{2,1,0:T(1,128)}), s32[16,1,64]{2,1,0:T(1,128)S(1)}, u32[]{:S(2)}, u32[]{:S(2)}) async-start(s32[16,1,64]{2,1,0:T(1,128)} %bitcast.19), calls=%async_computation.1 | async-start | bytes 16384 | tf_op jit(solution)/shard_map/all_to_all | solution.py:142
  30.8 1.2 copy-start.4
  33.6 9.2 %copy-start.7 = (bf16[64,2048]{1,0:T(8,128)(2,1)S(1)}, bf16[64,2048]{1,0:T(8,128)(2,1)}, u32[]{:S(2)}) copy-start(bf16[64,2048]{1,0:T(8,128)(2,1)} %param.10) | copy-start | bytes 786436
  33.7 57.5 %all-to-all-start = ((bf16[16,64,1024]{2,1,0:T(8,128)(2,1)}), bf16[16,64,1024]{2,1,0:T(8,128)(2,1)S(1)}, u32[]{:S(2)}, u32[]{:S(2)}) async-start(bf16[16,64,1024]{2,1,0:T(8,128)(2,1)} %pad_maximum_fusion), calls=%async_computation | async-start | bytes 4194304 | tf_op jit(solution)/shard_map/all_to_all | solution.py:16
  92.0 21.9 %all-to-all-start.2 = ((bf16[16,64,256]{2,1,0:T(8,128)(2,1)}), bf16[16,64,256]{2,1,0:T(8,128)(2,1)S(1)}, u32[]{:S(2)}, u32[]{:S(2)}) async-start(bf16[16,64,256]{2,1,0:T(8,128)(2,1)} %bitcast.215), calls=%async_computation.2 | async-start | bytes 1048576 | tf_op jit(solution)/shard_map/all_to_all | solution.py:152
  99.7 314.0 %all-reduce.2.cloned.1.call-start = ((), (), s32[]{:S(2)}) async-start(), calls=%async_computation.4 | async-start | bytes 2097152 | tf_op jit(solution)/shard_map/psum | solution.py:185
  120.4 7.5 %copy-start.1 = (f32[512,1024,4]{1,0,2:T(8,128)S(1)}, f32[512,1024,4]{1,0,2:T(8,128)}, u32[]{:S(2)}) copy-start(f32[512,1024,4]{1,0,2:T(8,128)} %get-tuple-element.204) | copy-start | bytes 25165828 | tf_op jit(solution)/shard_map/while
  136.5 8.0 %copy-start.1 = (f32[512,1024,4]{1,0,2:T(8,128)S(1)}, f32[512,1024,4]{1,0,2:T(8,128)}, u32[]{:S(2)}) copy-start(f32[512,1024,4]{1,0,2:T(8,128)} %get-tuple-element.204) | copy-start | bytes 25165828 | tf_op jit(solution)/shard_map/while
  146.7 2.4 copy-start.5
  149.2 1.2 copy-start.2
  150.4 1.6 copy-start.6
  158.4 1.0 copy-start.3
  160.1 15.0 %all-to-all-start.3 = ((f32[16,1,128]{2,1,0:T(1,128)}), f32[16,1,128]{2,1,0:T(1,128)S(1)}, u32[]{:S(2)}, u32[]{:S(2)}) async-start(f32[16,1,128]{2,1,0:T(1,128)} %bitcast.35), calls=%async_computation.3 | async-start | bytes 16384 | tf_op jit(solution)/shard_map/all_to_all | solution.py:16
Sparse Core Ops, SparseCore 0:
  159.5 254.1 all-reduce.1
where the time goes:
time: 426 us; the launch traced here: 425 us
  waiting for transfers between devices  304 us (71%)
  starting transfers between devices  35 us (8%)
  matrix products  31.6 us (7%)
  other arithmetic  20.2 us (5%)
  local copies, waits for them, and re-layouts  18.4 us (4%)
  between operations  15 us (4%)
    psum x1, waiting for transfers between devices, shards(): summed = lax.psum(flattened, ('blk', 'grp'))  238 us
    all_to_all x2, waiting for transfers between devices, sent_together(): lax.all_to_all(both, axis, split_axis=split_dim, concat_axis=concat_dim,...  56.7 us
    all_to_all x2, starting transfers between devices, sent_together(): lax.all_to_all(both, axis, split_axis=split_dim, concat_axis=concat_dim,...  15.5 us
    dot_general x2, matrix products, absorb(): jnp.einsum('rcgj,jcd->rcgd', raised.astype(jnp.bfloat16), value_part, pre...  15.5 us
    all_to_all x1, starting transfers between devices, shards(): lax.all_to_all(sent_limits, 'blk', split_axis=0, concat_axis=1, tiled=True)  11.6 us
    dot_general x2, matrix products, absorb(): jnp.einsum('rcgd,jcd->rcgj', teacher_q, key_part, preferred_element_type=...  9.63 us
    all_to_all x1, waiting for transfers between devices, shards(): lax.all_to_all(sent_cache, 'blk', split_axis=0, concat_axis=1, tiled=True)  9.57 us
    unnamed x22, local copies, waits for them, and re-layouts  9.13 us
  transfers between devices with their start and end apart: 5, of which 4 were waited for; matrix products, arithmetic and copies ran while one was open for 4% of the time, Pallas kernels for 0%

commit v1 on v0

v1 whole, which is shorter than its diff:
```python
import math

import jax
import jax.numpy as jnp
import numpy as np
from jax import lax
from jax.experimental import pallas as pl
from jax.experimental.pallas import tpu as pltpu
from jax.sharding import PartitionSpec as P

MESH = pl.DeviceIdType.MESH
rope_base = 500000.0
neg_fill = -1e30
norm_eps = 1e-06

HD = 128
KVH = 8
PER = 4
ROWS = 128
POS = 1024
SHARD = 64
PRE = 128
FEATURES = KVH * PER * HD
WIDE = PER * HD
KEYS = KVH * HD
SCALE = HD**-0.5
SCALE_LOG2E = SCALE * math.log2(math.e)

ORDER = (0, 1, 2, 3, 6, 7, 4, 5)


def coords():
    b, g = lax.axis_index("blk"), lax.axis_index("grp")
    return (b // 8) * 2 + g // 8, (g // 2) % 4, b % 8, g % 2


def device(x, y, z, c):
    return ((x // 2) * 8 + z, (x % 2) * 8 + y * 2 + c)


def sincos(angle):
    k = jnp.floor(angle * (2.0 / math.pi) + 0.5)
    r = angle - k * 1.5703125
    r = r - k * 4.837512969970703125e-4
    r = r - k * 7.54978995489188216e-8
    r2 = r * r
    s = r + r * r2 * (-1.6666654611e-1 + r2 * (8.3321608736e-3 + r2 * -1.9515295891e-4))
    c = 1.0 + r2 * (
        -0.5 + r2 * (4.166664568298827e-2 + r2 * (-1.388731625493765e-3 + r2 * 2.443315711809948e-5))
    )
    n = k.astype(jnp.int32)
    odd = (n & 1) == 1
    sine = jnp.where(odd, c, s)
    cosine = jnp.where(odd, s, c)
    sine = jnp.where((n & 2) == 2, -sine, sine)
    cosine = jnp.where(((n + 1) & 2) == 2, -cosine, cosine)
    return sine, cosine


def dot(a, b, ca, cb):
    return lax.dot_general(a, b, (((ca,), (cb,)), ((), ())), preferred_element_type=jnp.float32)


def rows_as_sublanes(row):
    return jnp.broadcast_to(row, (ROWS, ROWS)).T


def block_math(q, pos_row, lim_row, freq, keys, values, pk, pv):
    pos = rows_as_sublanes(pos_row.astype(jnp.float32))
    lim_f = rows_as_sublanes(lim_row.astype(jnp.float32))
    lane = lax.broadcasted_iota(jnp.int32, (ROWS, HD), 1)
    low = lane < HD // 2
    st, ct = sincos((lim_f + pos) * freq)
    ss, cs = sincos((PRE + pos) * freq)
    st = jnp.where(low, -st, st)
    ss = jnp.where(low, -ss, ss)
    lim = lim_f.astype(jnp.int32)
    student_q = []
    targets = []
    for h in range(PER):
        v = q[:, h * HD : (h + 1) * HD].astype(jnp.float32)
        vr = pltpu.roll(v, HD // 2, 1)
        student_q.append((v * cs + vr * ss).astype(jnp.bfloat16))
        tq = (v * ct + vr * st).astype(jnp.bfloat16)
        scores = dot(tq, keys, 1, 1)
        parts = []
        for j in range(POS // HD):
            part = scores[:, j * HD : (j + 1) * HD]
            if j >= 2:
                part = jnp.where(lane + j * HD < lim, part, neg_fill)
            parts.append(part)
        top = parts[0]
        for part in parts[1:]:
            top = jnp.maximum(top, part)
        top = jnp.max(top, axis=1, keepdims=True)
        total = None
        weights = []
        for part in parts:
            e = jnp.exp2((part - top) * SCALE_LOG2E)
            total = e if total is None else total + e
            weights.append(e.astype(jnp.bfloat16))
        total = jnp.sum(total, axis=1, keepdims=True)
        mixture = dot(jnp.concatenate(weights, axis=1), values, 1, 0)
        targets.append(mixture * (1.0 / total))
    sq = jnp.concatenate(student_q, axis=0)
    target = jnp.concatenate(targets, axis=0)
    scores = dot(sq, pk, 1, 1)
    raised = jnp.exp2((scores - jnp.max(scores, axis=1, keepdims=True)) * SCALE_LOG2E)
    probs = raised * (1.0 / jnp.sum(raised, axis=1, keepdims=True))
    rounded = probs.astype(jnp.bfloat16)
    out = dot(rounded, pv, 1, 0)
    diff = out - target
    cot = diff.astype(jnp.bfloat16)
    along = dot(cot, pv, 1, 1)
    inner = jnp.sum(probs * along, axis=1, keepdims=True)
    grad = (probs * (along - inner) * SCALE).astype(jnp.bfloat16)
    gv = dot(rounded, cot, 0, 0)
    gk = dot(grad, sq, 0, 0)
    d2 = diff * diff
    t2 = target * target
    dsum = d2[0:ROWS] + d2[ROWS : 2 * ROWS] + d2[2 * ROWS : 3 * ROWS] + d2[3 * ROWS :]
    tsum = t2[0:ROWS] + t2[ROWS : 2 * ROWS] + t2[2 * ROWS : 3 * ROWS] + t2[3 * ROWS :]
    derr = jnp.sum(dsum.T, axis=0, keepdims=True)
    terr = jnp.sum(tsum.T, axis=0, keepdims=True)
    return gk, gv, derr, terr


def kernel(
    q_hbm, pos_ref, lim_ref, cache_hbm, prefix_hbm, freq_ref,
    step_ref, err_ref,
    qbuf, ibuf, istage, kv, pbuf, grad, xland, xsum, zland, own8, eland, eout, nsend, nland, fin,
    local_sem, qs, qr, is_, ir, zs, zr, fs, fr, es, er, gxs, gxr, gzs, gzr, ps, pr, ns, nr,
):
    x, y, z, c = coords()
    x_hi, x_lo = x // 2, x % 2
    head = y * 2 + c

    def yc(k):
        return (y + k // 2) % 4, (c + k) % 2

    def yc_dev(k):
        yy, cc = yc(k)
        return device(x, yy, z, cc)

    def z_dev(k):
        return device(x, y, (z + k) % 8, c)

    def x_dev(k):
        return device((x + k) % 4, y, z, c)

    own_perm = z == head
    perm_dev = device(x, z // 2, head, z % 2)

    def remote(src, dst, ssem, rsem, dev):
        return pltpu.make_async_remote_copy(
            src_ref=src, dst_ref=dst, send_sem=ssem, recv_sem=rsem,
            device_id=dev, device_id_type=MESH,
        )

    def cols(start, n):
        return pl.ds(pl.multiple_of(start, HD), n)

    barrier = pltpu.get_barrier_semaphore()
    for k in range(1, 8):
        pl.semaphore_signal(barrier, inc=1, device_id=yc_dev(k), device_id_type=MESH)
        pl.semaphore_signal(barrier, inc=1, device_id=z_dev(k), device_id_type=MESH)
    for k in range(1, 4):
        pl.semaphore_signal(barrier, inc=1, device_id=x_dev(k), device_id_type=MESH)

    @pl.when(jnp.logical_not(own_perm))
    def _():
        pl.semaphore_signal(barrier, inc=1, device_id=perm_dev, device_id_type=MESH)

    own_rows = pl.ds(pl.multiple_of((x_hi * 8 + z) * SHARD, SHARD), SHARD)
    lc = [
        pltpu.make_async_copy(q_hbm.at[0, :, cols(head * WIDE, WIDE)], qbuf.at[head], local_sem.at[0]),
        pltpu.make_async_copy(
            cache_hbm.at[:, cols(x_lo * KEYS + head * HD, HD)], kv.at[x_lo, own_rows], local_sem.at[1]
        ),
        pltpu.make_async_copy(prefix_hbm.at[:, head], pbuf, local_sem.at[2]),
    ]
    for cp in lc:
        cp.start()
    istage[0:1, :] = pos_ref[...]
    istage[1:2, :] = lim_ref[...]
    ibuf[head, 0:1, :] = pos_ref[...]
    ibuf[head, 1:2, :] = lim_ref[...]

    pl.semaphore_wait(barrier, jnp.where(own_perm, 17, 18))

    lc[1].wait()
    zc = []
    for k in (1, 7, 2, 6, 3, 5, 4):
        cp = remote(kv.at[x_lo, own_rows], kv.at[x_lo, own_rows], zs.at[k], zr.at[k], z_dev(k))
        cp.start()
        zc.append(cp)
    qc = []
    for k in (1, 2, 3, 6, 7, 4, 5):
        yy, cc = yc(k)
        cp = remote(istage, ibuf.at[head], is_.at[k], ir.at[k], yc_dev(k))
        cp.start()
        qc.append(cp)
        cp = remote(
            q_hbm.at[0, :, cols((yy * 2 + cc) * WIDE, WIDE)], qbuf.at[head], qs.at[k], qr.at[k], yc_dev(k)
        )
        cp.start()
        qc.append(cp)
    for cp in zc:
        cp.wait()
    half = pl.ds(pl.multiple_of(x_hi * 512, 512), 512)
    fc = []
    for k in (1, 3, 2):
        cp = remote(kv.at[x_lo, half], kv.at[x_lo, half], fs.at[k], fr.at[k], x_dev(k))
        cp.start()
        fc.append(cp)
    lc[0].wait()
    lc[2].wait()
    for cp in fc:
        cp.wait()
    for cp in qc:
        cp.wait()

    freq = freq_ref[0:1, :]
    pk = pbuf[0]
    pv = pbuf[1]
    grad[...] = jnp.zeros_like(grad)

    def work(slot):
        gk, gv, derr, terr = block_math(
            qbuf[slot], ibuf[slot, 0:1, :], ibuf[slot, 1:2, :], freq, kv[0], kv[1], pk, pv
        )
        grad[0] += gk
        grad[1] += gv
        eout[slot, 0:1, :] = derr
        eout[slot, 1:2, :] = terr

    def body(i, carry):
        k = i
        work(((y + k // 2) % 4) * 2 + (c + k) % 2)
        return carry

    lax.fori_loop(0, 8, body, 0)

    gx = []
    for k in (1, 3, 2):
        xx = (x + k) % 4
        cp = remote(
            grad.at[xx // 2, pl.ds(pl.multiple_of((xx % 2) * 64, 64), 64)], xland.at[k], gxs.at[k], gxr.at[k], x_dev(k)
        )
        cp.start()
        gx.append(cp)
    ec = []
    for k in range(1, 8):
        yy, cc = yc(k)
        cp = remote(eout.at[yy * 2 + cc], eland.at[head], es.at[k], er.at[k], yc_dev(k))
        cp.start()
        ec.append(cp)
    eland[head] = eout[head]
    for cp in gx:
        cp.wait()
    xsum[...] = (
        grad[x_hi, pl.ds(pl.multiple_of(x_lo * 64, 64), 64), :] + xland[1] + xland[2] + xland[3]
    )
    gz = []
    for k in (4, 3, 5, 2, 6, 1, 7):
        zz = (z + k) % 8
        cp = remote(
            xsum.at[pl.ds(pl.multiple_of(zz * 8, 8), 8)], zland.at[k], gzs.at[k], gzr.at[k], z_dev(k)
        )
        cp.start()
        gz.append(cp)
    zland[0] = xsum[pl.ds(pl.multiple_of(z * 8, 8), 8), :]
    for cp in gz:
        cp.wait()
    rows8 = zland[0]
    for k in range(1, 8):
        rows8 = rows8 + zland[k]
    own8[...] = rows8

    @pl.when(jnp.logical_not(own_perm))
    def _():
        cp = remote(own8, fin, ps.at[0], pr.at[0], perm_dev)
        cp.start()

    @pl.when(own_perm)
    def _():
        fin[...] = own8[...]

    nsend[0] = jnp.broadcast_to(jnp.sum(rows8 * rows8, axis=0, keepdims=True), (8, HD))

    def exchange(stage, ks, dev):
        cps = []
        for k in ks:
            cp = remote(nsend.at[stage], nland.at[stage, k], ns.at[stage, k], nr.at[stage, k], dev(k))
            cp.start()
            cps.append(cp)
        for cp in cps:
            cp.wait()
        acc = nsend[stage]
        for k in ks:
            acc = acc + nland[stage, k]
        return acc

    nsend[1] = exchange(0, range(1, 8), yc_dev)
    nsend[2] = exchange(1, range(1, 4), x_dev)
    for cp in ec:
        cp.wait()
    esum = eland[0]
    for k in range(1, 8):
        esum = esum + eland[k]
    err_ref[...] = jnp.sqrt(esum[0:1] / FEATURES) / jnp.sqrt(esum[1:2] / FEATURES + norm_eps)

    @pl.when(jnp.logical_not(own_perm))
    def _():
        remote(own8, fin, ps.at[0], pr.at[0], perm_dev).wait()

    whole = exchange(2, range(1, 8), z_dev)
    mean_square = jnp.sum(whole, axis=1, keepdims=True) / (2.0 * KVH * PRE * HD)
    step_ref[...] = fin[...] / jnp.sqrt(mean_square + norm_eps)


def frequencies():
    f = (rope_base ** (-np.arange(HD // 2, dtype=np.float64) / (HD // 2))).astype(np.float32)
    return np.broadcast_to(np.concatenate([f, f])[None, :], (8, HD)).copy()


def shards(queries, question_pos, cache_limit, cache, prefix):
    freq = jnp.asarray(frequencies())
    vmem = pl.BlockSpec(memory_space=pltpu.VMEM)
    hbm = pl.BlockSpec(memory_space=pltpu.HBM)
    f32, bf16 = jnp.float32, jnp.bfloat16
    dma = pltpu.SemaphoreType.DMA
    return pl.pallas_call(
        kernel,
        out_shape=(
            jax.ShapeDtypeStruct((8, HD), f32),
            jax.ShapeDtypeStruct((1, ROWS), f32),
        ),
        in_specs=[hbm, vmem, vmem, hbm, hbm, vmem],
        out_specs=(vmem, vmem),
        scratch_shapes=[
            pltpu.VMEM((8, ROWS, WIDE), bf16),
            pltpu.VMEM((8, 8, ROWS), jnp.int32),
            pltpu.VMEM((8, ROWS), jnp.int32),
            pltpu.VMEM((2, POS, HD), bf16),
            pltpu.VMEM((2, PRE, HD), bf16),
            pltpu.VMEM((2, PRE, HD), f32),
            pltpu.VMEM((4, 64, HD), f32),
            pltpu.VMEM((64, HD), f32),
            pltpu.VMEM((8, 8, HD), f32),
            pltpu.VMEM((8, HD), f32),
            pltpu.VMEM((8, 8, ROWS), f32),
            pltpu.VMEM((8, 8, ROWS), f32),
            pltpu.VMEM((3, 8, HD), f32),
            pltpu.VMEM((3, 8, 8, HD), f32),
            pltpu.VMEM((8, HD), f32),
            dma((3,)),
            dma((8,)), dma((8,)), dma((8,)), dma((8,)), dma((8,)), dma((8,)), dma((4,)), dma((4,)),
            dma((8,)), dma((8,)), dma((4,)), dma((4,)), dma((8,)), dma((8,)), dma((1,)), dma((1,)),
            dma((3, 8)), dma((3, 8)),
        ],
        compiler_params=pltpu.CompilerParams(
            collective_id=0, has_side_effects=True, vmem_limit_bytes=48 * 1024 * 1024
        ),
        cost_estimate=pl.CostEstimate(
            flops=3_000_000_000, bytes_accessed=4_000_000, transcendentals=5_000_000
        ),
    )(queries, question_pos, cache_limit, cache, prefix, freq)


def solution(mesh):
    return jax.shard_map(
        shards,
        mesh=mesh,
        in_specs=(P("grp", "blk", None), P("grp", "blk"), P("grp", "blk"), P("blk", None), P()),
        out_specs=(P(("blk", "grp"), None), P("grp", "blk")),
        check_vma=False,
    )
```

time: 426 us -> 72.8 us (0.17)
  waiting for transfers between devices: 304 us -> 0 us
  Pallas kernels: 0 us -> 65.5 us
  starting transfers between devices: 35 us -> 0 us
  matrix products: 31.6 us -> 0 us
  other arithmetic: 20.2 us -> 0 us
  between operations: 15 us -> 0.65 us
  local copies, waits for them, and re-layouts: 18.4 us -> 6.31 us
    psum x1 -> x0, waiting for transfers between devices: 238 us -> none  [shards(): summed = lax.psum(flattened, ('blk', 'grp'))]
    all_to_all x4 -> x0, waiting for transfers between devices: 66.3 us -> none  [the longest x2 56.7 us: sent_together(): lax.all_to_all(both, axis, split_axis=split_dim, concat_axis=concat_dim,...]
    pallas_call x0 -> x1, Pallas kernels: none -> 65.5 us  [shards(): pl.pallas_call(kernel, out_shape=(jax.ShapeDtypeStruct((8, HD), f32), jax...]
    all_to_all x4 -> x0, starting transfers between devices: 34.8 us -> none  [the longest x2 15.5 us: sent_together(): lax.all_to_all(both, axis, split_axis=split_dim, concat_axis=concat_dim,...]
    dot_general x9 -> x0, matrix products: 31.6 us -> none  [the longest x2 15.5 us: absorb(): jnp.einsum('rcgj,jcd->rcgd', raised.astype(jnp.bfloat16), value_part, pre...]
    reduce_sum x7 -> x0, other arithmetic: 7.01 us -> none  [the longest x2 4.19 us: absorb(): totals = totals * factor + jnp.sum(raised, axis=-1)]
    concatenate x3 -> x0, other arithmetic: 4.42 us -> none  [the longest x2 2.29 us: sent_together(): both = jnp.concatenate(arrays, axis=along)]
    unnamed x22 -> x14, local copies, waits for them, and re-layouts: 9.13 us -> 6.31 us
  transfers between devices with their start and end apart: 5 -> 0, of which waited for: 4 -> 0; matrix products, arithmetic and copies ran while one was open for 4% -> 0% of each run, Pallas kernels for 0% -> 0%
where the time goes in v1:
time: 72.8 us; the launch traced here: 72.5 us
  Pallas kernels  65.5 us (90%)
  local copies, waits for them, and re-layouts  6.31 us (9%)
    pallas_call x1, Pallas kernels, shards(): pl.pallas_call(kernel, out_shape=(jax.ShapeDtypeStruct((8, HD), f32), jax...  65.5 us
    unnamed x14, local copies, waits for them, and re-layouts  6.31 us

profile of v1, /device:TPU:1, one launch (start us, length us, event | category | flops | bytes accessed | tf_op | source)
XLA Modules:
  0.0 72.5 jit_solution(2488242958737389273)
XLA Ops:
  0.6 0.0 copy-start
  0.6 1.2 %copy-done = bf16[1,128,4096]{2,1,0:T(8,128)(2,1)S(1)} copy-done((bf16[1,128,4096]{2,1,0:T(8,128)(2,1)S(1)}, bf16[1,128,4096]{2,1,0:T(8,128)(2,1)}, u32[]{:S(2)}) %copy-start) | copy-done | bytes 1048600
  1.9 0.0 copy-start.1
  1.9 1.0 %copy-done.1 = bf16[2,8,128,128]{3,2,1,0:T(8,128)(2,1)S(1)} copy-done((bf16[2,8,128,128]{3,2,1,0:T(8,128)(2,1)S(1)}, bf16[2,8,128,128]{3,2,1,0:T(8,128)(2,1)}, u32[]{:S(2)}) %copy-start.1) | copy-done | bytes 524312
  2.9 0.0 copy-start.2
  2.9 0.9 %copy-done.2 = bf16[64,2048]{1,0:T(8,128)(2,1)S(1)} copy-done((bf16[64,2048]{1,0:T(8,128)(2,1)S(1)}, bf16[64,2048]{1,0:T(8,128)(2,1)}, u32[]{:S(2)}) %copy-start.2) | copy-done | bytes 262168
  3.8 0.0 copy-start.3
  3.9 0.7 copy-done.3
  4.5 0.0 copy-start.4
  4.5 0.7 copy-done.4
  5.2 0.0 copy-start.5
  5.2 0.7 copy-done.5
  5.8 65.5 %shard_map.77 = (f32[8,128]{1,0:T(8,128)S(1)}, f32[1,128]{1,0:T(1,128)S(1)}) custom-call(bf16[1,128,4096]{2,1,0:T(8,128)(2,1)S(1)} %copy-done, s32[1,128]{1,0:T(1,128)S(1)} %copy-done.3, s32[1,128]{1,0:T(1,128)S(1)} %copy-done.4, bf16[64,2048]{1,0:T(8,128)(2,1)S(1)} %copy-done.2, bf16[2,8,128,128]{3,2,1,0:T(8,128)(2,1)S(1)} %copy-done.1, f32[8,128]{1,0:T(8,128)S(1)} %copy-done.5), custom_call_target="tpu_custom_call" | custom-call | flops 3000000000 | bytes 4000000 | tf_op jit(solution)/shard_map/pallas_call | solution.py:333
  71.4 0.6 copy.10
  72.0 0.5 copy.11
Async XLA Ops:
  0.6 1.2 %copy-start = (bf16[1,128,4096]{2,1,0:T(8,128)(2,1)S(1)}, bf16[1,128,4096]{2,1,0:T(8,128)(2,1)}, u32[]{:S(2)}) copy-start(bf16[1,128,4096]{2,1,0:T(8,128)(2,1)} %q_hbm.1) | copy-start | bytes 3145732
  1.9 1.0 %copy-start.1 = (bf16[2,8,128,128]{3,2,1,0:T(8,128)(2,1)S(1)}, bf16[2,8,128,128]{3,2,1,0:T(8,128)(2,1)}, u32[]{:S(2)}) copy-start(bf16[2,8,128,128]{3,2,1,0:T(8,128)(2,1)} %prefix_hbm.1) | copy-start | bytes 1572868
  2.9 0.9 %copy-start.2 = (bf16[64,2048]{1,0:T(8,128)(2,1)S(1)}, bf16[64,2048]{1,0:T(8,128)(2,1)}, u32[]{:S(2)}) copy-start(bf16[64,2048]{1,0:T(8,128)(2,1)} %cache_hbm.1) | copy-start | bytes 786436
  3.8 0.7 copy-start.3
  4.5 0.7 copy-start.4
  5.2 0.7 copy-start.5

commit v2 on v1

v2 whole, which is shorter than its diff:
```python
import math

import jax
import jax.numpy as jnp
import numpy as np
from jax import lax
from jax.experimental import pallas as pl
from jax.experimental.pallas import tpu as pltpu
from jax.sharding import PartitionSpec as P

MESH = pl.DeviceIdType.MESH
rope_base = 500000.0
neg_fill = -1e30
norm_eps = 1e-06

HD = 128
KVH = 8
PER = 4
ROWS = 128
POS = 1024
SHARD = 64
PRE = 128
FEATURES = KVH * PER * HD
WIDE = PER * HD
KEYS = KVH * HD
SCALE = HD**-0.5
SCALE_LOG2E = SCALE * math.log2(math.e)


def coords():
    b, g = lax.axis_index("blk"), lax.axis_index("grp")
    return (b // 8) * 2 + g // 8, (g // 2) % 4, b % 8, g % 2


def device(x, y, z, c):
    return ((x // 2) * 8 + z, (x % 2) * 8 + y * 2 + c)


def sincos(angle):
    k = jnp.floor(angle * (2.0 / math.pi) + 0.5)
    r = angle - k * 1.5703125
    r = r - k * 4.837512969970703125e-4
    r = r - k * 7.54978995489188216e-8
    r2 = r * r
    s = r + r * r2 * (-1.6666654611e-1 + r2 * (8.3321608736e-3 + r2 * -1.9515295891e-4))
    c = 1.0 + r2 * (
        -0.5 + r2 * (4.166664568298827e-2 + r2 * (-1.388731625493765e-3 + r2 * 2.443315711809948e-5))
    )
    n = k.astype(jnp.int32)
    odd = (n & 1) == 1
    sine = jnp.where(odd, c, s)
    cosine = jnp.where(odd, s, c)
    sine = jnp.where((n & 2) == 2, -sine, sine)
    cosine = jnp.where(((n + 1) & 2) == 2, -cosine, cosine)
    return sine, cosine


def dot(a, b, ca, cb):
    return lax.dot_general(a, b, (((ca,), (cb,)), ((), ())), preferred_element_type=jnp.float32)


RC = 256
JC = 256

def teacher(q, pos_row, lim_row, freq_col, keys, values_t, eye):
    pos = pos_row.astype(jnp.float32)
    lim = lim_row.astype(jnp.float32)
    half = HD // 2
    st, ct = sincos(freq_col * (lim + pos))
    ss, cs = sincos(freq_col * (PRE + pos))
    qt = [dot(eye, q[:, h * HD : (h + 1) * HD], 1, 1) for h in range(PER)]
    def turned(cosine, sine):
        parts = []
        for h in range(PER):
            lead, trail = qt[h][:half], qt[h][half:]
            parts.append(
                jnp.concatenate(
                    [lead * cosine - trail * sine, trail * cosine + lead * sine], axis=0
                ).astype(jnp.bfloat16)
            )
        return parts
    tq = turned(ct, st)
    sq = turned(cs, ss)
    targets = []
    for r in range(0, PER, RC // HD):
        n = RC // HD
        part_q = jnp.concatenate(tq[r : r + n], axis=1)
        limits = jnp.concatenate([lim_row] * n, axis=1)
        parts = []
        top = None
        for j in range(0, POS, JC):
            part = dot(keys[j : j + JC], part_q, 1, 0)
            if j >= 256:
                where = lax.broadcasted_iota(jnp.int32, (JC, RC), 0) + j
                part = jnp.where(where < limits, part, neg_fill)
            parts.append(part)
            m = jnp.max(part, axis=0, keepdims=True)
            top = m if top is None else jnp.maximum(top, m)
        total = None
        mixture = None
        for a, part in enumerate(parts):
            e = jnp.exp2((part - top) * SCALE_LOG2E)
            t = jnp.sum(e, axis=0, keepdims=True)
            total = t if total is None else total + t
            o = dot(values_t[:, a * JC : (a + 1) * JC], e.astype(jnp.bfloat16), 1, 0)
            mixture = o if mixture is None else mixture + o
        targets.append(mixture * (1.0 / total))
    return jnp.concatenate(targets, axis=1), jnp.concatenate(sq, axis=1)

def student(sq, target, pk, pv, pv_t):
    scores = dot(pk, sq, 1, 0)
    raised = jnp.exp2((scores - jnp.max(scores, axis=0, keepdims=True)) * SCALE_LOG2E)
    probs = raised * (1.0 / jnp.sum(raised, axis=0, keepdims=True))
    rounded = probs.astype(jnp.bfloat16)
    out = dot(pv_t, rounded, 1, 0)
    diff = out - target
    cot = diff.astype(jnp.bfloat16)
    along = dot(pv, cot, 1, 0)
    inner = jnp.sum(probs * along, axis=0, keepdims=True)
    grad = (probs * (along - inner) * SCALE).astype(jnp.bfloat16)
    gv = dot(rounded, cot, 1, 1)
    gk = dot(grad, sq, 1, 1)
    d = jnp.sum(diff * diff, axis=0, keepdims=True)
    t = jnp.sum(target * target, axis=0, keepdims=True)
    return gk, gv, d, t

def heads_sum(d):
    return d[:, :ROWS] + d[:, ROWS : 2 * ROWS] + d[:, 2 * ROWS : 3 * ROWS] + d[:, 3 * ROWS :]


def far_first(k):
    dx, dz = k // 8, k % 8
    return -(min(dx, 4 - dx) + min(dz, 8 - dz))


PLANE = sorted(range(1, 32), key=far_first)


def kernel(
    q_hbm, pos_hbm, lim_hbm, cache_hbm, prefix_hbm, freq_hbm,
    step_ref, err_ref,
    qbuf, ibuf, istage, freq, kv, vt, pbuf, pvt, eye, grad, rland, own8, eland, eout, nsend, nyc, nxz, fin,
    local_sem, qs, qr, is_, ir, zs, zr, fs, fr, es, er, gs, gr, ps, pr, ns, nr,
):
    x, y, z, c = coords()
    x_hi, x_lo = x // 2, x % 2
    head = y * 2 + c

    def yc(k):
        return (y + k // 2) % 4, (c + k) % 2

    def yc_dev(k):
        yy, cc = yc(k)
        return device(x, yy, z, cc)

    def z_dev(k):
        return device(x, y, (z + k) % 8, c)

    def x_dev(k):
        return device((x + k) % 4, y, z, c)

    def xz(k):
        return (x + k // 8) % 4, (z + k % 8) % 8

    def xz_dev(k):
        xx, zz = xz(k)
        return device(xx, y, zz, c)

    own_perm = z == head
    perm_dev = device(x, z // 2, head, z % 2)

    def remote(src, dst, ssem, rsem, dev):
        return pltpu.make_async_remote_copy(
            src_ref=src, dst_ref=dst, send_sem=ssem, recv_sem=rsem,
            device_id=dev, device_id_type=MESH,
        )

    def cols(start, n):
        return pl.ds(pl.multiple_of(start, HD), n)

    def shard_rows(zz):
        return pl.ds(pl.multiple_of((x_hi * 8 + zz) * SHARD, SHARD), SHARD)

    barrier = pltpu.get_barrier_semaphore()
    for k in range(1, 8):
        pl.semaphore_signal(barrier, inc=1, device_id=z_dev(k), device_id_type=MESH)
        pl.semaphore_signal(barrier, inc=1, device_id=yc_dev(k), device_id_type=MESH)
    for k in range(1, 4):
        pl.semaphore_signal(barrier, inc=1, device_id=x_dev(k), device_id_type=MESH)

    own_rows = shard_rows(z)
    lc = [
        pltpu.make_async_copy(
            cache_hbm.at[:, cols(x_lo * KEYS + head * HD, HD)], kv.at[x_lo, own_rows], local_sem.at[0]
        ),
        pltpu.make_async_copy(pos_hbm, istage.at[pl.ds(0, 1)], local_sem.at[1]),
        pltpu.make_async_copy(lim_hbm, istage.at[pl.ds(1, 1)], local_sem.at[2]),
        pltpu.make_async_copy(q_hbm.at[0, :, cols(head * WIDE, WIDE)], qbuf.at[head], local_sem.at[3]),
        pltpu.make_async_copy(prefix_hbm.at[:, head], pbuf, local_sem.at[4]),
        pltpu.make_async_copy(freq_hbm, freq, local_sem.at[5]),
    ]
    for cp in lc:
        cp.start()
    grad[...] = jnp.zeros_like(grad)
    eye[...] = jnp.where(
        lax.broadcasted_iota(jnp.int32, (HD, HD), 0) == lax.broadcasted_iota(jnp.int32, (HD, HD), 1), 1.0, 0.0
    ).astype(jnp.bfloat16)
    lc[0].wait()
    lc[1].wait()
    lc[2].wait()

    pl.semaphore_wait(barrier, 17)

    sent = []
    zc = {}
    for k in (1, 7, 2, 6, 3, 5, 4):
        zc[k] = remote(kv.at[x_lo, own_rows], kv.at[x_lo, own_rows], zs.at[k], zr.at[k], z_dev(k))
        zc[k].start()
        sent.append(zc[k])
    fc = []

    def forward(k):
        rows = shard_rows((z + 8 - k) % 8)
        for n in (1, 3, 2):
            cp = remote(kv.at[x_lo, rows], kv.at[x_lo, rows], fs.at[k, n], fr.at[k, n], x_dev(n))
            cp.start()
            fc.append(cp)
            sent.append(cp)

    forward(0)
    for k in (1, 2, 3, 6, 7, 4, 5):
        yy, cc = yc(k)
        cp = remote(istage, ibuf.at[head], is_.at[k], ir.at[k], yc_dev(k))
        cp.start()
        sent.append(cp)
        cp = remote(
            q_hbm.at[0, :, cols((yy * 2 + cc) * WIDE, WIDE)], qbuf.at[head], qs.at[k], qr.at[k], yc_dev(k)
        )
        cp.start()
        sent.append(cp)
    for k in (1, 7, 2, 6, 3, 5, 4):
        zc[k].wait_recv()
        forward(k)
    ibuf[head] = istage[...]
    lc[3].wait()
    lc[4].wait()
    lc[5].wait()
    pvt[...] = pbuf[1].T
    for cp in fc:
        cp.wait_recv()
    vt[...] = kv[1].T

    def body(p, carry):
        dy = p ^ (p >> 1)
        kk = ((4 - dy) % 4) * 2
        base = ((y + dy) % 4) * 2
        a, b = base + c, base + 1 - c

        @pl.when(p > 0)
        def _():
            remote(istage, ibuf.at[a], is_.at[kk], ir.at[kk], yc_dev(2)).wait_recv()
            remote(qbuf.at[a], qbuf.at[a], qs.at[kk], qr.at[kk], yc_dev(2)).wait_recv()

        remote(istage, ibuf.at[b], is_.at[kk + 1], ir.at[kk + 1], yc_dev(2)).wait_recv()
        remote(qbuf.at[b], qbuf.at[b], qs.at[kk + 1], qr.at[kk + 1], yc_dev(2)).wait_recv()
        ts, ss = [], []
        for slot in (a, b):
            t, s = teacher(
                qbuf[slot], ibuf[slot, 0:1, :], ibuf[slot, 1:2, :], freq[...], kv[0], vt[...], eye[...]
            )
            ts.append(t)
            ss.append(s)
        gk, gv, d, t = student(
            jnp.concatenate(ss, axis=1), jnp.concatenate(ts, axis=1), pbuf[0], pbuf[1], pvt[...]
        )
        grad[0] += gk
        grad[1] += gv
        for n, slot in enumerate((a, b)):
            eout[slot, 0:1, :] = heads_sum(d[:, n * WIDE : (n + 1) * WIDE])
            eout[slot, 1:2, :] = heads_sum(t[:, n * WIDE : (n + 1) * WIDE])
        return carry

    lax.fori_loop(0, 4, body, 0)

    for k in PLANE:
        xx, zz = xz(k)
        src = grad.at[xx // 2, pl.ds(pl.multiple_of((xx % 2) * 64 + zz * 8, 8), 8)]
        remote(src, rland.at[k], gs, gr, xz_dev(k)).start()
    for k in range(1, 8):
        yy, cc = yc(k)
        cp = remote(eout.at[yy * 2 + cc], eland.at[head], es.at[k], er.at[k], yc_dev(k))
        cp.start()
        sent.append(cp)
    eland[head] = eout[head]
    rows8 = grad[x_hi, pl.ds(pl.multiple_of(x_lo * 64 + z * 8, 8), 8), :]
    all31 = rland.at[pl.ds(1, 31)]
    remote(all31, all31, gs, gr, xz_dev(1)).wait_recv()
    for k in range(1, 32):
        rows8 = rows8 + rland[k]
    own8[...] = rows8
    nsend[0:1] = jnp.sum(rows8 * rows8, axis=0, keepdims=True)
    ycs = []
    for k in (4, 5, 2, 3, 6, 7, 1):
        cp = remote(nsend.at[pl.ds(0, 1)], nyc.at[pl.ds(k, 1)], ns.at[0], nr.at[0], yc_dev(k))
        cp.start()

    @pl.when(jnp.logical_not(own_perm))
    def _():
        remote(own8, fin, ps.at[0], pr.at[0], perm_dev).start()

    @pl.when(own_perm)
    def _():
        fin[...] = own8[...]

    nyc[0:1] = nsend[0:1]
    seven = nyc.at[pl.ds(1, 7)]
    remote(seven, seven, ns.at[0], nr.at[0], yc_dev(1)).wait_recv()
    nsend[1:2] = jnp.sum(nyc[...], axis=0, keepdims=True)
    for k in PLANE:
        remote(nsend.at[pl.ds(1, 1)], nxz.at[pl.ds(k, 1)], ns.at[1], nr.at[1], xz_dev(k)).start()
    nxz[0:1] = nsend[1:2]
    for k in range(1, 8):
        remote(eout.at[k], eland.at[k], es.at[k], er.at[k], yc_dev(k)).wait_recv()
    esum = eland[0]
    for k in range(1, 8):
        esum = esum + eland[k]
    err_ref[...] = jnp.sqrt(esum[0:1] / FEATURES) / jnp.sqrt(esum[1:2] / FEATURES + norm_eps)
    for cp in sent:
        cp.wait_send()
    remote(all31, all31, gs, gr, xz_dev(1)).wait_send()
    remote(seven, seven, ns.at[0], nr.at[0], yc_dev(1)).wait_send()

    @pl.when(jnp.logical_not(own_perm))
    def _():
        remote(own8, fin, ps.at[0], pr.at[0], perm_dev).wait()

    thirty = nxz.at[pl.ds(1, 31)]
    remote(thirty, thirty, ns.at[1], nr.at[1], xz_dev(1)).wait()
    whole = jnp.sum(nxz[...], axis=0, keepdims=True)
    mean_square = jnp.sum(whole, axis=1, keepdims=True) / (2.0 * KVH * PRE * HD)
    step_ref[...] = fin[...] / jnp.sqrt(mean_square + norm_eps)


def frequencies():
    f = (rope_base ** (-np.arange(HD // 2, dtype=np.float64) / (HD // 2))).astype(np.float32)
    return np.broadcast_to(f[:, None], (HD // 2, ROWS)).copy()


def shards(queries, question_pos, cache_limit, cache, prefix):
    freq = jnp.asarray(frequencies())
    vmem = pl.BlockSpec(memory_space=pltpu.VMEM)
    hbm = pl.BlockSpec(memory_space=pltpu.HBM)
    f32, bf16 = jnp.float32, jnp.bfloat16
    dma = pltpu.SemaphoreType.DMA
    return pl.pallas_call(
        kernel,
        out_shape=(
            jax.ShapeDtypeStruct((8, HD), f32),
            jax.ShapeDtypeStruct((1, ROWS), f32),
        ),
        in_specs=[hbm] * 6,
        out_specs=(vmem, vmem),
        scratch_shapes=[
            pltpu.VMEM((8, ROWS, WIDE), bf16),
            pltpu.VMEM((8, 8, ROWS), jnp.int32),
            pltpu.VMEM((8, ROWS), jnp.int32),
            pltpu.VMEM((HD // 2, ROWS), f32),
            pltpu.VMEM((2, POS, HD), bf16),
            pltpu.VMEM((HD, POS), bf16),
            pltpu.VMEM((2, PRE, HD), bf16),
            pltpu.VMEM((HD, PRE), bf16),
            pltpu.VMEM((HD, HD), bf16),
            pltpu.VMEM((2, PRE, HD), f32),
            pltpu.VMEM((32, 8, HD), f32),
            pltpu.VMEM((8, HD), f32),
            pltpu.VMEM((8, 8, ROWS), f32),
            pltpu.VMEM((8, 8, ROWS), f32),
            pltpu.VMEM((8, HD), f32),
            pltpu.VMEM((8, HD), f32),
            pltpu.VMEM((32, HD), f32),
            pltpu.VMEM((8, HD), f32),
            dma((6,)),
            dma((8,)), dma((8,)), dma((8,)), dma((8,)), dma((8,)), dma((8,)), dma((8, 4)), dma((8, 4)),
            dma((8,)), dma((8,)), dma, dma, dma((1,)), dma((1,)), dma((2,)), dma((2,)),
        ],
        compiler_params=pltpu.CompilerParams(
            collective_id=0, has_side_effects=True, vmem_limit_bytes=60 * 1024 * 1024
        ),
        cost_estimate=pl.CostEstimate(
            flops=3_000_000_000, bytes_accessed=4_000_000, transcendentals=5_000_000
        ),
    )(queries, question_pos, cache_limit, cache, prefix, freq)


def solution(mesh):
    return jax.shard_map(
        shards,
        mesh=mesh,
        in_specs=(P("grp", "blk", None), P("grp", "blk"), P("grp", "blk"), P("blk", None), P()),
        out_specs=(P(("blk", "grp"), None), P("grp", "blk")),
        check_vma=False,
    )
```

time: 72.8 us -> 50.9 us (0.70)
  Pallas kernels: 65.5 us -> 48.4 us
  local copies, waits for them, and re-layouts: 6.31 us -> 1.78 us
    pallas_call x1, Pallas kernels: 65.5 us -> 48.4 us  [shards(): pl.pallas_call(kernel, out_shape=(jax.ShapeDtypeStruct((8, HD), f32), jax...]
    unnamed x14 -> x4, local copies, waits for them, and re-layouts: 6.31 us -> 1.78 us
where the time goes in v2:
time: 50.9 us; the launch traced here: 50.8 us
  Pallas kernels  48.4 us (95%)
  local copies, waits for them, and re-layouts  1.78 us (3%)
  between operations  0.65 us (1%)
    pallas_call x1, Pallas kernels, shards(): pl.pallas_call(kernel, out_shape=(jax.ShapeDtypeStruct((8, HD), f32), jax...  48.4 us
    unnamed x4, local copies, waits for them, and re-layouts  1.78 us

profile of v2, /device:TPU:1, one launch (start us, length us, event | category | flops | bytes accessed | tf_op | source)
XLA Modules:
  0.0 50.8 jit_solution(18017925523737877110)
XLA Ops:
  0.6 48.4 %shard_map.77 = (f32[8,128]{1,0:T(8,128)}, f32[1,128]{1,0:T(1,128)}) custom-call(bf16[1,128,4096]{2,1,0:T(8,128)(2,1)} %q_hbm.1, s32[1,128]{1,0:T(1,128)} %pos_hbm.1, s32[1,128]{1,0:T(1,128)} %lim_hbm.1, bf16[64,2048]{1,0:T(8,128)(2,1)} %cache_hbm.1, bf16[2,8,128,128]{3,2,1,0:T(8,128)(2,1)} %prefix_hbm.1, f32[64,128]{1,0:T(8,128)} %constant.2.clone.freq_hbm), custom_call_target="tpu_custom_call" | custom-call | flops 3000000000 | bytes 4000000 | tf_op jit(solution)/shard_map/pallas_call | solution.py:355
  49.0 0.0 copy-start
  49.0 1.3 %copy.10 = f32[8,128]{1,0:T(8,128)} copy(f32[8,128]{1,0:T(8,128)} %get-tuple-element.4) | data formatting | bytes 8192
  50.3 0.0 copy-done
  50.3 0.5 %copy.11 = f32[1,128]{1,0:T(1,128)} copy(f32[1,128]{1,0:T(1,128)S(1)} %copy-done) | data formatting | bytes 1024
Async XLA Ops:
  49.0 1.3 %copy-start = (f32[1,128]{1,0:T(1,128)S(1)}, f32[1,128]{1,0:T(1,128)}, u32[]{:S(2)}) copy-start(f32[1,128]{1,0:T(1,128)} %get-tuple-element.5) | copy-start | bytes 1540

commit v3 on v2

v3 whole, which is shorter than its diff:
```python
import math

import jax
import jax.numpy as jnp
import numpy as np
from jax import lax
from jax.experimental import pallas as pl
from jax.experimental.pallas import tpu as pltpu
from jax.sharding import PartitionSpec as P

MESH = pl.DeviceIdType.MESH
rope_base = 500000.0
neg_fill = -1e30
norm_eps = 1e-06

HD = 128
KVH = 8
PER = 4
ROWS = 128
POS = 1024
SHARD = 64
PRE = 128
FEATURES = KVH * PER * HD
WIDE = PER * HD
KEYS = KVH * HD
SCALE = HD**-0.5
JC = 256
SCALE_LOG2E = SCALE * math.log2(math.e)


def sincos(angle):
    k = jnp.floor(angle * (2.0 / math.pi) + 0.5)
    r = angle - k * 1.5703125
    r = r - k * 4.837512969970703125e-4
    r = r - k * 7.54978995489188216e-8
    r2 = r * r
    s = r + r * r2 * (-1.6666654611e-1 + r2 * (8.3321608736e-3 + r2 * -1.9515295891e-4))
    c = 1.0 + r2 * (
        -0.5 + r2 * (4.166664568298827e-2 + r2 * (-1.388731625493765e-3 + r2 * 2.443315711809948e-5))
    )
    n = k.astype(jnp.int32)
    odd = (n & 1) == 1
    sine = jnp.where(odd, c, s)
    cosine = jnp.where(odd, s, c)
    sine = jnp.where((n & 2) == 2, -sine, sine)
    cosine = jnp.where(((n + 1) & 2) == 2, -cosine, cosine)
    return sine, cosine


def dot(a, b, ca, cb):
    return lax.dot_general(a, b, (((ca,), (cb,)), ((), ())), preferred_element_type=jnp.float32)


def prepare(q, pos_row, lim_row, freq_col, eye):
    pos = pos_row.astype(jnp.float32)
    lim = lim_row.astype(jnp.float32)
    half = HD // 2
    st, ct = sincos(freq_col * (lim + pos))
    ss, cs = sincos(freq_col * (PRE + pos))
    tq, sq = [], []
    for h in range(PER):
        qt = dot(eye, q[:, h * HD : (h + 1) * HD], 1, 1)
        lead, trail = qt[:half], qt[half:]
        for cosine, sine, out in ((ct, st, tq), (cs, ss, sq)):
            out.append(
                jnp.concatenate(
                    [lead * cosine - trail * sine, trail * cosine + lead * sine], axis=0
                ).astype(jnp.bfloat16)
            )
    return jnp.concatenate(tq, axis=1), jnp.concatenate(sq, axis=1)


def teacher(tq, lim_row, keys, values_t):
    limits = jnp.concatenate([lim_row] * PER, axis=1)
    parts = []
    top = None
    for j in range(0, POS, JC):
        part = dot(keys[j : j + JC], tq, 1, 0)
        if j >= 256:
            where = lax.broadcasted_iota(jnp.int32, part.shape, 0) + j
            part = jnp.where(where < limits, part, neg_fill)
        parts.append(part)
        m = jnp.max(part, axis=0, keepdims=True)
        top = m if top is None else jnp.maximum(top, m)
    total = None
    mixture = None
    for a, part in enumerate(parts):
        e = jnp.exp2((part - top) * SCALE_LOG2E)
        t = jnp.sum(e, axis=0, keepdims=True)
        total = t if total is None else total + t
        o = dot(values_t[:, a * JC : (a + 1) * JC], e.astype(jnp.bfloat16), 1, 0)
        mixture = o if mixture is None else mixture + o
    return mixture * (1.0 / total)


def student_forward(sq, pk, pv_t):
    scores = dot(pk, sq, 1, 0)
    raised = jnp.exp2((scores - jnp.max(scores, axis=0, keepdims=True)) * SCALE_LOG2E)
    probs = raised * (1.0 / jnp.sum(raised, axis=0, keepdims=True))
    rounded = probs.astype(jnp.bfloat16)
    return probs, rounded, dot(pv_t, rounded, 1, 0)


def student_backward(sq, probs, rounded, out, target, pv):
    diff = out - target
    cot = diff.astype(jnp.bfloat16)
    along = dot(pv, cot, 1, 0)
    inner = jnp.sum(probs * along, axis=0, keepdims=True)
    grad = (probs * (along - inner) * SCALE).astype(jnp.bfloat16)
    gv = dot(rounded, cot, 1, 1)
    gk = dot(grad, sq, 1, 1)
    d = jnp.sum(diff * diff, axis=0, keepdims=True)
    t = jnp.sum(target * target, axis=0, keepdims=True)
    return gk, gv, d, t


def heads_sum(d):
    return d[:, :ROWS] + d[:, ROWS : 2 * ROWS] + d[:, 2 * ROWS : 3 * ROWS] + d[:, 3 * ROWS :]


HOPS = (0, 1, 2, 3, 4, 3, 2, 1)
PLANE = sorted(range(1, 32), key=lambda k: -(HOPS[k % 8] + (0, 1, 2, 1)[k // 8]))


def kernel(
    q_hbm, pos_hbm, lim_hbm, cache_hbm, prefix_hbm, freq_hbm,
    step_ref, err_ref,
    qbuf, ibuf, istage, freq, kv, vt, pbuf, pvt, eye, grad, rland, own8, eland, eout, nsend, nyc, nxz, fin,
    tqs, sqs, probs, rounded, outs,
    local_sem, qs, qr, is_, ir, zs, zr, fs, fr, es, er, gs, gr, ps, pr, ns, nr,
):
    blk, grp = lax.axis_index("blk"), lax.axis_index("grp")
    x_hi, z = blk // 8, blk % 8
    x_lo, head = grp // 8, grp % 8
    piece = x_hi * 16 + x_lo * 8 + z

    def yc_dev(k):
        return (blk, grp ^ k)

    def xz_dev(k):
        n = k // 8
        return (blk ^ ((n // 2) * 8 + k % 8), grp ^ ((n % 2) * 8) if n % 2 else grp)

    own_perm = z == head
    perm_dev = (x_hi * 8 + head, x_lo * 8 + z)

    def remote(src, dst, ssem, rsem, dev):
        return pltpu.make_async_remote_copy(
            src_ref=src, dst_ref=dst, send_sem=ssem, recv_sem=rsem,
            device_id=dev, device_id_type=MESH,
        )

    def cols(start, n):
        return pl.ds(pl.multiple_of(start, HD), n)

    def shard_rows(k):
        return pl.ds(pl.multiple_of((blk ^ k) * SHARD, SHARD), SHARD)

    def piece_rows(k):
        return pl.ds(pl.multiple_of((piece ^ k) * 8, 8), 8)

    barrier = pltpu.get_barrier_semaphore()
    for k in (4, 5, 3, 7, 2, 6, 1):
        pl.semaphore_signal(barrier, inc=1, device_id=xz_dev(k), device_id_type=MESH)
    for k in (16, 8, 24):
        pl.semaphore_signal(barrier, inc=1, device_id=xz_dev(k), device_id_type=MESH)
    for k in (4, 5, 2, 3, 6, 7, 1):
        pl.semaphore_signal(barrier, inc=1, device_id=yc_dev(k), device_id_type=MESH)

    own_rows = shard_rows(0)
    lc = [
        pltpu.make_async_copy(
            cache_hbm.at[:, cols(x_lo * KEYS + head * HD, HD)], kv.at[x_lo, own_rows], local_sem.at[0]
        ),
        pltpu.make_async_copy(pos_hbm, istage.at[pl.ds(0, 1)], local_sem.at[1]),
        pltpu.make_async_copy(lim_hbm, istage.at[pl.ds(1, 1)], local_sem.at[2]),
        pltpu.make_async_copy(q_hbm.at[0, :, cols(head * WIDE, WIDE)], qbuf.at[head], local_sem.at[3]),
        pltpu.make_async_copy(prefix_hbm.at[:, head], pbuf, local_sem.at[4]),
        pltpu.make_async_copy(freq_hbm, freq, local_sem.at[5]),
    ]
    for cp in lc:
        cp.start()
    eye[...] = jnp.where(
        lax.broadcasted_iota(jnp.int32, (HD, HD), 0) == lax.broadcasted_iota(jnp.int32, (HD, HD), 1), 1.0, 0.0
    ).astype(jnp.bfloat16)
    for cp in lc[:3]:
        cp.wait()

    pl.semaphore_wait(barrier, 17)

    sent = []
    zc = {}
    for k in (1, 7, 3, 2, 6, 5, 4):
        zc[k] = remote(kv.at[x_lo, own_rows], kv.at[x_lo, own_rows], zs.at[k], zr.at[k], xz_dev(k))
        zc[k].start()
        sent.append(zc[k])
    fc = []

    def forward(k):
        rows = shard_rows(k)
        for n in (2, 1, 3):
            cp = remote(kv.at[x_lo, rows], kv.at[x_lo, rows], fs.at[k, n], fr.at[k, n], xz_dev(8 * n))
            cp.start()
            fc.append(cp)
            sent.append(cp)

    qc = {}

    def send_rows(k):
        a = remote(istage, ibuf.at[head], is_.at[k], ir.at[k], yc_dev(k))
        a.start()
        b = remote(q_hbm.at[0, :, cols((head ^ k) * WIDE, WIDE)], qbuf.at[head], qs.at[k], qr.at[k], yc_dev(k))
        b.start()
        qc[k] = (a, b)
        sent.extend(qc[k])

    forward(0)
    for k in (1, 2, 3, 6, 7, 4, 5):
        send_rows(k)
    for k in (1, 7, 3, 2, 6, 5, 4):
        zc[k].wait_recv()
        forward(k)
    ibuf[head] = istage[...]
    for cp in lc[3:]:
        cp.wait()
    pvt[...] = pbuf[1].T

    def arrive(k):
        for cp in qc[k]:
            cp.wait_recv()

    def prep(i, k):
        s = head ^ k
        t, u = prepare(qbuf[s], ibuf[s, 0:1, :], ibuf[s, 1:2, :], freq[...], eye[...])
        tqs[:, i * WIDE : (i + 1) * WIDE] = t
        sqs[:, i * WIDE : (i + 1) * WIDE] = u

    def ahead():
        p, r, o = student_forward(sqs[...], pbuf[0], pvt[...])
        probs[...] = p
        rounded[...] = r
        outs[...] = o

    def rest(ks):
        target = jnp.concatenate(
            [
                teacher(tqs[:, i * WIDE : (i + 1) * WIDE], ibuf[head ^ k, 1:2, :], kv[0], vt[...])
                for i, k in enumerate(ks)
            ],
            axis=1,
        )
        gk, gv, d, t = student_backward(sqs[...], probs[...], rounded[...], outs[...], target, pbuf[1])
        for i, k in enumerate(ks):
            eout[head ^ k, 0:1, :] = heads_sum(d[:, i * WIDE : (i + 1) * WIDE])
            eout[head ^ k, 1:2, :] = heads_sum(t[:, i * WIDE : (i + 1) * WIDE])
        return gk, gv

    first, second = (0, 1, 2, 3), (6, 7, 4, 5)
    prep(0, 0)
    for i, k in enumerate(first[1:]):
        arrive(k)
        prep(i + 1, k)
    ahead()
    for cp in fc:
        cp.wait_recv()
    vt[...] = kv[1].T
    gk, gv = rest(first)
    grad[0:PRE] = gk
    grad[PRE:] = gv
    for k in second:
        arrive(k)
    for i, k in enumerate(second):
        prep(i, k)
    ahead()
    gk, gv = rest(second)
    grad[0:PRE] += gk
    grad[PRE:] += gv

    for k in PLANE:
        remote(grad.at[piece_rows(k)], rland.at[k], gs, gr, xz_dev(k)).start()
    for k in range(1, 8):
        cp = remote(eout.at[head ^ k], eland.at[head], es.at[k], er.at[k], yc_dev(k))
        cp.start()
        sent.append(cp)
    eland[head] = eout[head]
    rows8 = grad[piece_rows(0), :]
    all31 = rland.at[pl.ds(1, 31)]
    remote(all31, all31, gs, gr, xz_dev(1)).wait_recv()
    for k in range(1, 32):
        rows8 = rows8 + rland[k]
    own8[...] = rows8
    nsend[0:1] = jnp.sum(rows8 * rows8, axis=0, keepdims=True)
    for k in (4, 5, 2, 3, 6, 7, 1):
        remote(nsend.at[pl.ds(0, 1)], nyc.at[pl.ds(k, 1)], ns.at[0], nr.at[0], yc_dev(k)).start()

    @pl.when(jnp.logical_not(own_perm))
    def _():
        remote(own8, fin, ps.at[0], pr.at[0], perm_dev).start()

    @pl.when(own_perm)
    def _():
        fin[...] = own8[...]

    nyc[0:1] = nsend[0:1]
    seven = nyc.at[pl.ds(1, 7)]
    remote(seven, seven, ns.at[0], nr.at[0], yc_dev(1)).wait_recv()
    nsend[1:2] = jnp.sum(nyc[...], axis=0, keepdims=True)
    for k in PLANE:
        remote(nsend.at[pl.ds(1, 1)], nxz.at[pl.ds(k, 1)], ns.at[1], nr.at[1], xz_dev(k)).start()
    nxz[0:1] = nsend[1:2]
    for k in range(1, 8):
        remote(eout.at[k], eland.at[k], es.at[k], er.at[k], yc_dev(k)).wait_recv()
    esum = eland[0]
    for k in range(1, 8):
        esum = esum + eland[k]
    err_ref[...] = jnp.sqrt(esum[0:1] / FEATURES) / jnp.sqrt(esum[1:2] / FEATURES + norm_eps)
    for cp in sent:
        cp.wait_send()
    remote(all31, all31, gs, gr, xz_dev(1)).wait_send()
    remote(seven, seven, ns.at[0], nr.at[0], yc_dev(1)).wait_send()

    @pl.when(jnp.logical_not(own_perm))
    def _():
        remote(own8, fin, ps.at[0], pr.at[0], perm_dev).wait()

    thirty = nxz.at[pl.ds(1, 31)]
    remote(thirty, thirty, ns.at[1], nr.at[1], xz_dev(1)).wait()
    whole = jnp.sum(nxz[...], axis=0, keepdims=True)
    mean_square = jnp.sum(whole, axis=1, keepdims=True) / (2.0 * KVH * PRE * HD)
    step_ref[...] = fin[...] / jnp.sqrt(mean_square + norm_eps)


def frequencies():
    f = (rope_base ** (-np.arange(HD // 2, dtype=np.float64) / (HD // 2))).astype(np.float32)
    return np.broadcast_to(f[:, None], (HD // 2, ROWS)).copy()


def shards(queries, question_pos, cache_limit, cache, prefix):
    freq = jnp.asarray(frequencies())
    vmem = pl.BlockSpec(memory_space=pltpu.VMEM)
    hbm = pl.BlockSpec(memory_space=pltpu.HBM)
    f32, bf16 = jnp.float32, jnp.bfloat16
    dma = pltpu.SemaphoreType.DMA
    return pl.pallas_call(
        kernel,
        out_shape=(
            jax.ShapeDtypeStruct((8, HD), f32),
            jax.ShapeDtypeStruct((1, ROWS), f32),
        ),
        in_specs=[hbm] * 6,
        out_specs=(vmem, vmem),
        scratch_shapes=[
            pltpu.VMEM((8, ROWS, WIDE), bf16),
            pltpu.VMEM((8, 8, ROWS), jnp.int32),
            pltpu.VMEM((8, ROWS), jnp.int32),
            pltpu.VMEM((HD // 2, ROWS), f32),
            pltpu.VMEM((2, POS, HD), bf16),
            pltpu.VMEM((HD, POS), bf16),
            pltpu.VMEM((2, PRE, HD), bf16),
            pltpu.VMEM((HD, PRE), bf16),
            pltpu.VMEM((HD, HD), bf16),
            pltpu.VMEM((2 * PRE, HD), f32),
            pltpu.VMEM((32, 8, HD), f32),
            pltpu.VMEM((8, HD), f32),
            pltpu.VMEM((8, 8, ROWS), f32),
            pltpu.VMEM((8, 8, ROWS), f32),
            pltpu.VMEM((8, HD), f32),
            pltpu.VMEM((8, HD), f32),
            pltpu.VMEM((32, HD), f32),
            pltpu.VMEM((8, HD), f32),
            pltpu.VMEM((HD, 4 * WIDE), bf16),
            pltpu.VMEM((HD, 4 * WIDE), bf16),
            pltpu.VMEM((PRE, 4 * WIDE), f32),
            pltpu.VMEM((PRE, 4 * WIDE), bf16),
            pltpu.VMEM((HD, 4 * WIDE), f32),
            dma((6,)),
            dma((8,)), dma((8,)), dma((8,)), dma((8,)), dma((8,)), dma((8,)), dma((8, 4)), dma((8, 4)),
            dma((8,)), dma((8,)), dma, dma, dma((1,)), dma((1,)), dma((2,)), dma((2,)),
        ],
        compiler_params=pltpu.CompilerParams(
            collective_id=0, has_side_effects=True, vmem_limit_bytes=60 * 1024 * 1024
        ),
        cost_estimate=pl.CostEstimate(
            flops=3_000_000_000, bytes_accessed=4_000_000, transcendentals=5_000_000
        ),
    )(queries, question_pos, cache_limit, cache, prefix, freq)


def solution(mesh):
    return jax.shard_map(
        shards,
        mesh=mesh,
        in_specs=(P("grp", "blk", None), P("grp", "blk"), P("grp", "blk"), P("blk", None), P()),
        out_specs=(P(("blk", "grp"), None), P("grp", "blk")),
        check_vma=False,
    )
```

time: 50.9 us -> 48.6 us (0.955)
  Pallas kernels: 48.4 us -> 46 us
    pallas_call x1, Pallas kernels: 48.4 us -> 46 us  [shards(): pl.pallas_call(kernel, out_shape=(jax.ShapeDtypeStruct((8, HD), f32), jax...]
where the time goes in v3:
time: 48.6 us; the launch traced here: 48.4 us
  Pallas kernels  46 us (95%)
  local copies, waits for them, and re-layouts  1.78 us (4%)
  between operations  0.65 us (1%)
    pallas_call x1, Pallas kernels, shards(): pl.pallas_call(kernel, out_shape=(jax.ShapeDtypeStruct((8, HD), f32), jax...  46 us
    unnamed x4, local copies, waits for them, and re-layouts  1.78 us

profile of v3, /device:TPU:1, one launch (start us, length us, event | category | flops | bytes accessed | tf_op | source)
XLA Modules:
  0.0 48.4 jit_solution(1201506257274339576)
XLA Ops:
  0.6 46.0 %shard_map.77 = (f32[8,128]{1,0:T(8,128)}, f32[1,128]{1,0:T(1,128)}) custom-call(bf16[1,128,4096]{2,1,0:T(8,128)(2,1)} %q_hbm.1, s32[1,128]{1,0:T(1,128)} %pos_hbm.1, s32[1,128]{1,0:T(1,128)} %lim_hbm.1, bf16[64,2048]{1,0:T(8,128)(2,1)} %cache_hbm.1, bf16[2,8,128,128]{3,2,1,0:T(8,128)(2,1)} %prefix_hbm.1, f32[64,128]{1,0:T(8,128)} %constant.2.clone.freq_hbm), custom_call_target="tpu_custom_call" | custom-call | flops 3000000000 | bytes 4000000 | tf_op jit(solution)/shard_map/pallas_call | solution.py:344
  46.7 0.0 copy-start
  46.7 1.3 %copy.10 = f32[8,128]{1,0:T(8,128)} copy(f32[8,128]{1,0:T(8,128)} %get-tuple-element.4) | data formatting | bytes 8192
  47.9 0.0 copy-done
  47.9 0.5 %copy.11 = f32[1,128]{1,0:T(1,128)} copy(f32[1,128]{1,0:T(1,128)S(1)} %copy-done) | data formatting | bytes 1024
Async XLA Ops:
  46.7 1.3 %copy-start = (f32[1,128]{1,0:T(1,128)S(1)}, f32[1,128]{1,0:T(1,128)}, u32[]{:S(2)}) copy-start(f32[1,128]{1,0:T(1,128)} %get-tuple-element.5) | copy-start | bytes 1540

commit v4 on v3

--- a/solution.py
+++ b/solution.py
@@ -71,7 +71,7 @@
 
 
 def teacher(tq, lim_row, keys, values_t):
-    limits = jnp.concatenate([lim_row] * PER, axis=1)
+    limits = lim_row
     parts = []
     top = None
     for j in range(0, POS, JC):
@@ -244,8 +244,13 @@
     def rest(ks):
         target = jnp.concatenate(
             [
-                teacher(tqs[:, i * WIDE : (i + 1) * WIDE], ibuf[head ^ k, 1:2, :], kv[0], vt[...])
-                for i, k in enumerate(ks)
+                teacher(
+                    tqs[:, i * WIDE : (i + 2) * WIDE],
+                    jnp.concatenate([ibuf[head ^ ks[i], 1:2, :]] * PER + [ibuf[head ^ ks[i + 1], 1:2, :]] * PER, axis=1),
+                    kv[0],
+                    vt[...],
+                )
+                for i in range(0, len(ks), 2)
             ],
             axis=1,
         )

time: 48.6 us -> 48 us (0.988)
  Pallas kernels: 46 us -> 45.4 us
    pallas_call x1, Pallas kernels: 46 us -> 45.4 us  [shards(): pl.pallas_call(kernel, out_shape=(jax.ShapeDtypeStruct((8, HD), f32), jax...]
where the time goes in v4:
time: 48 us; the launch traced here: 47.8 us
  Pallas kernels  45.4 us (95%)
  local copies, waits for them, and re-layouts  1.78 us (4%)
  between operations  0.65 us (1%)
    pallas_call x1, Pallas kernels, shards(): pl.pallas_call(kernel, out_shape=(jax.ShapeDtypeStruct((8, HD), f32), jax...  45.4 us
    unnamed x4, local copies, waits for them, and re-layouts  1.78 us

profile of v4, /device:TPU:1, one launch (start us, length us, event | category | flops | bytes accessed | tf_op | source)
XLA Modules:
  0.0 47.8 jit_solution(10953644318081510767)
XLA Ops:
  0.6 45.4 %shard_map.77 = (f32[8,128]{1,0:T(8,128)}, f32[1,128]{1,0:T(1,128)}) custom-call(bf16[1,128,4096]{2,1,0:T(8,128)(2,1)} %q_hbm.1, s32[1,128]{1,0:T(1,128)} %pos_hbm.1, s32[1,128]{1,0:T(1,128)} %lim_hbm.1, bf16[64,2048]{1,0:T(8,128)(2,1)} %cache_hbm.1, bf16[2,8,128,128]{3,2,1,0:T(8,128)(2,1)} %prefix_hbm.1, f32[64,128]{1,0:T(8,128)} %constant.2.clone.freq_hbm), custom_call_target="tpu_custom_call" | custom-call | flops 3000000000 | bytes 4000000 | tf_op jit(solution)/shard_map/pallas_call | solution.py:349
  46.1 0.0 copy-start
  46.1 1.3 %copy.10 = f32[8,128]{1,0:T(8,128)} copy(f32[8,128]{1,0:T(8,128)} %get-tuple-element.4) | data formatting | bytes 8192
  47.3 0.0 copy-done
  47.3 0.5 %copy.11 = f32[1,128]{1,0:T(1,128)} copy(f32[1,128]{1,0:T(1,128)S(1)} %copy-done) | data formatting | bytes 1024
Async XLA Ops:
  46.1 1.3 %copy-start = (f32[1,128]{1,0:T(1,128)S(1)}, f32[1,128]{1,0:T(1,128)}, u32[]{:S(2)}) copy-start(f32[1,128]{1,0:T(1,128)} %get-tuple-element.5) | copy-start | bytes 1540

commit v5 on v4

--- a/solution.py
+++ b/solution.py
@@ -199,7 +199,7 @@
     def forward(k):
         rows = shard_rows(k)
         for n in (2, 1, 3):
-            cp = remote(kv.at[x_lo, rows], kv.at[x_lo, rows], fs.at[k, n], fr.at[k, n], xz_dev(8 * n))
+            cp = remote(kv.at[x_lo, rows], kv.at[x_lo, rows], fs.at[k, n], fr, xz_dev(8 * n))
             cp.start()
             fc.append(cp)
             sent.append(cp)
@@ -266,8 +266,8 @@
         arrive(k)
         prep(i + 1, k)
     ahead()
-    for cp in fc:
-        cp.wait_recv()
+    three = qbuf.at[pl.ds(0, 3)]
+    remote(three, three, fs.at[0, 1], fr, xz_dev(8)).wait_recv()
     vt[...] = kv[1].T
     gk, gv = rest(first)
     grad[0:PRE] = gk
@@ -379,7 +379,7 @@
             pltpu.VMEM((PRE, 4 * WIDE), bf16),
             pltpu.VMEM((HD, 4 * WIDE), f32),
             dma((6,)),
-            dma((8,)), dma((8,)), dma((8,)), dma((8,)), dma((8,)), dma((8,)), dma((8, 4)), dma((8, 4)),
+            dma((8,)), dma((8,)), dma((8,)), dma((8,)), dma((8,)), dma((8,)), dma((8, 4)), dma,
             dma((8,)), dma((8,)), dma, dma, dma((1,)), dma((1,)), dma((2,)), dma((2,)),
         ],
         compiler_params=pltpu.CompilerParams(

time: 48 us -> 47.7 us (level)
  no operation moved by 1% of the time
where the time goes in v5:
time: 47.7 us; the launch traced here: 47.6 us
  Pallas kernels  45.1 us (95%)
  local copies, waits for them, and re-layouts  1.78 us (4%)
  between operations  0.65 us (1%)
    pallas_call x1, Pallas kernels, shards(): pl.pallas_call(kernel, out_shape=(jax.ShapeDtypeStruct((8, HD), f32), jax...  45.1 us
    unnamed x4, local copies, waits for them, and re-layouts  1.78 us

profile of v5, /device:TPU:1, one launch (start us, length us, event | category | flops | bytes accessed | tf_op | source)
XLA Modules:
  0.0 47.6 jit_solution(15403599149279197021)
XLA Ops:
  0.6 45.1 %shard_map.77 = (f32[8,128]{1,0:T(8,128)}, f32[1,128]{1,0:T(1,128)}) custom-call(bf16[1,128,4096]{2,1,0:T(8,128)(2,1)} %q_hbm.1, s32[1,128]{1,0:T(1,128)} %pos_hbm.1, s32[1,128]{1,0:T(1,128)} %lim_hbm.1, bf16[64,2048]{1,0:T(8,128)(2,1)} %cache_hbm.1, bf16[2,8,128,128]{3,2,1,0:T(8,128)(2,1)} %prefix_hbm.1, f32[64,128]{1,0:T(8,128)} %constant.2.clone.freq_hbm), custom_call_target="tpu_custom_call" | custom-call | flops 3000000000 | bytes 4000000 | tf_op jit(solution)/shard_map/pallas_call | solution.py:349
  45.8 0.0 copy-start
  45.8 1.3 %copy.10 = f32[8,128]{1,0:T(8,128)} copy(f32[8,128]{1,0:T(8,128)} %get-tuple-element.4) | data formatting | bytes 8192
  47.0 0.0 copy-done
  47.0 0.5 %copy.11 = f32[1,128]{1,0:T(1,128)} copy(f32[1,128]{1,0:T(1,128)S(1)} %copy-done) | data formatting | bytes 1024
Async XLA Ops:
  45.8 1.3 %copy-start = (f32[1,128]{1,0:T(1,128)S(1)}, f32[1,128]{1,0:T(1,128)}, u32[]{:S(2)}) copy-start(f32[1,128]{1,0:T(1,128)} %get-tuple-element.5) | copy-start | bytes 1540

commit v6 on v5

--- a/solution.py
+++ b/solution.py
@@ -198,7 +198,7 @@
 
     def forward(k):
         rows = shard_rows(k)
-        for n in (2, 1, 3):
+        for n in (2, 3, 1):
             cp = remote(kv.at[x_lo, rows], kv.at[x_lo, rows], fs.at[k, n], fr, xz_dev(8 * n))
             cp.start()
             fc.append(cp)

time: 47.7 us -> 47.7 us (level)
  no operation moved by 1% of the time
where the time goes in v6:
time: 47.7 us; the launch traced here: 47.6 us
  Pallas kernels  45.1 us (95%)
  local copies, waits for them, and re-layouts  1.78 us (4%)
  between operations  0.65 us (1%)
    pallas_call x1, Pallas kernels, shards(): pl.pallas_call(kernel, out_shape=(jax.ShapeDtypeStruct((8, HD), f32), jax...  45.1 us
    unnamed x4, local copies, waits for them, and re-layouts  1.78 us

profile of v6, /device:TPU:1, one launch (start us, length us, event | category | flops | bytes accessed | tf_op | source)
XLA Modules:
  0.0 47.6 jit_solution(13112205642581061197)
XLA Ops:
  0.6 45.1 %shard_map.77 = (f32[8,128]{1,0:T(8,128)}, f32[1,128]{1,0:T(1,128)}) custom-call(bf16[1,128,4096]{2,1,0:T(8,128)(2,1)} %q_hbm.1, s32[1,128]{1,0:T(1,128)} %pos_hbm.1, s32[1,128]{1,0:T(1,128)} %lim_hbm.1, bf16[64,2048]{1,0:T(8,128)(2,1)} %cache_hbm.1, bf16[2,8,128,128]{3,2,1,0:T(8,128)(2,1)} %prefix_hbm.1, f32[64,128]{1,0:T(8,128)} %constant.2.clone.freq_hbm), custom_call_target="tpu_custom_call" | custom-call | flops 3000000000 | bytes 4000000 | tf_op jit(solution)/shard_map/pallas_call | solution.py:349
  45.8 0.0 copy-start
  45.8 1.3 %copy.10 = f32[8,128]{1,0:T(8,128)} copy(f32[8,128]{1,0:T(8,128)} %get-tuple-element.4) | data formatting | bytes 8192
  47.0 0.0 copy-done
  47.0 0.5 %copy.11 = f32[1,128]{1,0:T(1,128)} copy(f32[1,128]{1,0:T(1,128)S(1)} %copy-done) | data formatting | bytes 1024
Async XLA Ops:
  45.8 1.3 %copy-start = (f32[1,128]{1,0:T(1,128)S(1)}, f32[1,128]{1,0:T(1,128)}, u32[]{:S(2)}) copy-start(f32[1,128]{1,0:T(1,128)} %get-tuple-element.5) | copy-start | bytes 1540
